TPU v7x, 512 devices: a whole 4x8x8 slice. The times are simulated.
512 devices in a mesh: row: 32 (over z, x), inw: 8 (over y_lo, core), outw: 2 (over y_hi).
Axes of the slice: x: 4, y: 8 (y_hi: 2, y_lo: 4; y = y_hi * 4 + y_lo), z: 8, core: 2. Of those that a mesh axis runs over, the one named last changes fastest.
Arguments:
- inputs: bfloat16 [768, 8192], P('row', ('inw', 'outw')), may hold values from -6 to 6
- out_grad: bfloat16 [768, 8192], P('row', ('inw', 'outw')), may hold values from -3 to 3
- gate_weight: bfloat16 [8192, 16384], P(('inw', 'outw'), 'row'), may hold values from -0.0625 to 0.0625
- up_weight: bfloat16 [8192, 16384], P(('inw', 'outw'), 'row'), may hold values from -0.0625 to 0.0625
- down_weight: bfloat16 [16384, 8192], P('row', ('inw', 'outw')), may hold values from -0.046875 to 0.046875
Outputs:
- grad_inputs: bfloat16 [768, 8192], P('row', ('inw', 'outw'))
- grad_gate: bfloat16 [8192, 16384], P(('inw', 'outw'), 'row')
- grad_up: bfloat16 [8192, 16384], P(('inw', 'outw'), 'row')
- grad_down: bfloat16 [16384, 8192], P('row', ('inw', 'outw'))
All inputs are finite; a program needn't handle non-finite values.
Results may differ from a plain program's by a relative error of at most 0.0049.
Values may be sent and summed in bfloat16 or wider, within the bound.
A program may use at most 64 MiB of HBM per device.

v0:
```python
import jax
import jax.numpy as jnp
from jax import lax
from jax.sharding import PartitionSpec as P


def contract_last(left, right):
    return lax.dot_general(
        left, right, (((1,), (1,)), ((), ())), preferred_element_type=jnp.float32
    )


def contract_first(left, right):
    return lax.dot_general(
        left, right, (((0,), (0,)), ((), ())), preferred_element_type=jnp.float32
    )


def swiglu_grads(gate_sum, up_sum, back_sum):
    sigmoid_gate = jax.nn.sigmoid(gate_sum)
    silu_gate = gate_sum * sigmoid_gate
    hidden = (silu_gate * up_sum).astype(jnp.bfloat16)
    gate_grad = (back_sum * up_sum * sigmoid_gate * (1.0 + gate_sum * (1.0 - sigmoid_gate))).astype(
        jnp.bfloat16
    )
    up_grad = (back_sum * silu_gate).astype(jnp.bfloat16)
    return (hidden, gate_grad, up_grad)


def per_device(inputs, out_grad, gate_weight, up_weight, down_weight):
    input_rows, grad_rows = (
        lax.all_gather(inputs, "row", axis=0, tiled=True),
        lax.all_gather(out_grad, "row", axis=0, tiled=True),
    )
    gate_part = jnp.dot(input_rows, gate_weight, preferred_element_type=jnp.float32)
    up_part = jnp.dot(input_rows, up_weight, preferred_element_type=jnp.float32)
    back_part = contract_last(grad_rows, down_weight)
    gate_sum, up_sum, back_sum = lax.psum((gate_part, up_part, back_part), ("inw", "outw"))
    hidden, gate_grad, up_grad = swiglu_grads(gate_sum, up_sum, back_sum)
    grad_down = contract_first(hidden, grad_rows).astype(jnp.bfloat16)
    grad_gate = contract_first(input_rows, gate_grad).astype(jnp.bfloat16)
    grad_up = contract_first(input_rows, up_grad).astype(jnp.bfloat16)
    grad_inputs = lax.psum_scatter(
        contract_last(gate_grad, gate_weight) + contract_last(up_grad, up_weight),
        "row",
        scatter_dimension=0,
        tiled=True,
    ).astype(jnp.bfloat16)
    return (grad_inputs, grad_gate, grad_up, grad_down)


def solution(mesh):
    in_specs = (
        P("row", ("inw", "outw")),
        P("row", ("inw", "outw")),
        P(("inw", "outw"), "row"),
        P(("inw", "outw"), "row"),
        P("row", ("inw", "outw")),
    )
    out_specs = (
        P("row", ("inw", "outw")),
        P(("inw", "outw"), "row"),
        P(("inw", "outw"), "row"),
        P("row", ("inw", "outw")),
    )
    return jax.shard_map(
        per_device, mesh=mesh, in_specs=in_specs, out_specs=out_specs, check_vma=False
    )
```

profile of v0, /device:TPU:1, one launch (start us, length us, event | category | flops | bytes accessed | tf_op | source)
XLA Modules:
  0.0 475.0 jit_solution(17125121648859528537)
XLA Ops:
  7.2 0.0 copy-start
  7.2 0.0 all-reduce.3.cloned.1.call-start
  7.2 44.7 %all_gather.7 = bf16[768,512]{1,0:T(8,128)(2,1)S(1)} all-gather(bf16[24,512]{1,0:T(8,128)(2,1)} %param.5), channel_id=1, replica_groups=mesh['row'=32,'inw'=8,'outw'=2] {'row'}, dimensions={0}, use_global_device_ids=true | all-gather | bytes 811008 | tf_op jit(solution)/shard_map/all_gather | solution.py:32
  51.9 37.2 %all_gather.6 = bf16[768,512]{1,0:T(8,128)(2,1)S(1)} all-gather(bf16[24,512]{1,0:T(8,128)(2,1)} %param.6), channel_id=1, replica_groups=mesh['row'=32,'inw'=8,'outw'=2] {'row'}, dimensions={0}, use_global_device_ids=true | all-gather | bytes 811008 | tf_op jit(solution)/shard_map/all_gather | solution.py:33
  89.1 0.0 copy-done
  89.1 1.7 fusion.7
  90.8 0.0 copy-done.2
  90.8 1.8 fusion.6
  92.6 1.7 fusion.5
  94.4 0.0 all-reduce.3.cloned.1.call-update
  94.4 0.0 reduce-scatter.2.cloned.1.call-start
  94.4 148.1 %all-reduce.3.cloned.1.call-done = (f32[768,512]{1,0:T(8,128)}, f32[768,512]{1,0:T(8,128)}, f32[768,512]{1,0:T(8,128)}) async-done(((f32[768,512]{1,0:T(8,128)}, f32[768,512]{1,0:T(8,128)}, f32[768,512]{1,0:T(8,128)}), (f32[768,512]{1,0:T(8,128)}, f32[768,512]{1,0:T(8,128)}, f32[768,512]{1,0:T(8,128)})) %all-reduce.3.cloned.1.call-update) | async-done | bytes 4718608 | tf_op jit(solution)/shard_map/psum | solution.py:38
  242.5 3.2 multiply_convert_fusion.1
  245.8 0.6 fusion.8
  246.4 0.3 copy-done.1
  246.7 1.8 convolution_add_fusion
  248.4 0.0 reduce-scatter.2.cloned.1.call-update
  248.5 0.6 fusion.1
  249.1 1.0 copy.9
  250.1 1.7 fusion.2
  251.8 1.0 copy.10
  252.8 3.3 convolution_convert_fusion
  256.1 210.6 %reduce-scatter.2.cloned.1.call-done = f32[24,512]{1,0:T(8,128)} async-done(((f32[768,512]{1,0:T(8,128)}), f32[24,512]{1,0:T(8,128)}) %reduce-scatter.2.cloned.1.call-update) | async-done | bytes 49168 | tf_op jit(solution)/shard_map/reduce_scatter | solution.py:43
  466.7 1.4 convert_element_type.29
  (4 shorter events, 0.0 us)
Async XLA Ops:
  7.2 81.9 %copy-start = (bf16[512,512]{1,0:T(8,128)(2,1)S(1)}, bf16[512,512]{1,0:T(8,128)(2,1)}, u32[]{:S(2)}) copy-start(bf16[512,512]{1,0:T(8,128)(2,1)} %param.7) | copy-start | bytes 1572868
  7.2 235.3 %all-reduce.3.cloned.1.call-start = ((), (), s32[]{:S(2)}) async-start(), calls=%async_computation.2 | async-start | bytes 9437184 | tf_op jit(solution)/shard_map/psum | solution.py:38
  89.1 1.7 copy-start.2
  90.8 1.8 copy-start.3
  94.4 372.3 %reduce-scatter.2.cloned.1.call-start = ((), (), s32[]{:S(2)}) async-start(), calls=%async_computation.1 | async-start | bytes 1622016 | tf_op jit(solution)/shard_map/reduce_scatter | solution.py:43
  245.7 0.9 copy-start.1
Sparse Core Ops, SparseCore 0:
  94.5 147.9 all-reduce.2
  248.6 218.1 reduce-scatter.1
where the time goes:
time: 480 us; the launch traced here: 475 us
  waiting for transfers between devices  359 us (75%)
  blocking collectives  81.8 us (17%)
  between operations  14.1 us (3%)
  matrix products  13.3 us (3%)
    reduce_scatter x1, waiting for transfers between devices, per_device(): lax.psum_scatter(contract_last(gate_grad, gate_weight) + contract_last(up...  211 us
    psum x1, waiting for transfers between devices, per_device(): lax.psum((gate_part, up_part, back_part), ('inw', 'outw'))  148 us
    all_gather x1, blocking collectives, per_device(): lax.all_gather(inputs, 'row', axis=0, tiled=True)  44.7 us
    all_gather x1, blocking collectives, per_device(): lax.all_gather(out_grad, 'row', axis=0, tiled=True)  37.2 us
  transfers between devices with their start and end apart: 2, of which 2 were waited for; matrix products, arithmetic and copies ran while one was open for 2% of the time, Pallas kernels for 0%

commit v1 on v0

v1 whole, which is shorter than its diff:
```python
import functools

import jax
import jax.numpy as jnp
from jax import lax
from jax.experimental import pallas as pl
from jax.experimental.pallas import tpu as pltpu
from jax.sharding import PartitionSpec as P

MESH = pl.DeviceIdType.MESH
BF, F32 = jnp.bfloat16, jnp.float32
NZ, NX, NY = 8, 4, 8
GROUPS = {0: ((0, 1), (2,)), 1: ((0, 1, 2),), 2: ((0, 1, 2),), 3: ((0, 1, 2),)}


def dot(a, b):
    return jnp.dot(a, b, preferred_element_type=F32)


def dot_nt(a, b):
    return lax.dot_general(a, b, (((1,), (1,)), ((), ())), preferred_element_type=F32)


def dot_tn(a, b):
    return lax.dot_general(a, b, (((0,), (0,)), ((), ())), preferred_element_type=F32)


def scratch(t, w, f):
    made = {
        "xb": ((NX, NZ, t, w), BF),
        "gb": ((NX, NZ, t, w), BF),
        "wg": ((2, w, f), BF),
        "wu": ((2, w, f), BF),
        "wd": ((2, f, w), BF),
        "hb": ((2, NX, NZ, 3, t, f), BF),
        "dxs": ((NX, NZ, t, w), F32),
        "dxr": ((NX, NZ, t, w), F32),
        "zs": ((NZ, t, w), BF),
        "zr": ((NZ, t, w), BF),
        "og": ((2, w, f), BF),
        "ou": ((2, w, f), BF),
        "od": ((2, f, w), BF),
    }
    for c, groups in GROUPS.items():
        for g, qs in enumerate(groups):
            n = len(qs)
            made[f"po{c}{g}"] = ((NZ, n, t, f), F32)
            made[f"cs{c}{g}"] = ((NZ, n, t, f), F32)
            made[f"cr{c}{g}"] = ((NZ, n, t, f), F32)
            made[f"pb{c}{g}"] = ((NZ, n, t, f), BF)
            made[f"rr{c}{g}"] = ((3, n, t, f), BF)
            made[f"sr{c}{g}"] = ((2, n, t, f), BF)
            made[f"ro{c}{g}"] = ((4, n, t, f), BF)
    return made


N_REMOTE = 160
N_LOCAL = 16


def kernel(names, x_ref, g_ref, wg_hbm, wu_hbm, wd_hbm, dx_ref, og_hbm, ou_hbm, od_hbm, *refs):
    buf = dict(zip(names, refs))
    ssem, rsem, lsem = refs[len(names) :]
    t, w = x_ref.shape
    f = wg_hbm.shape[1] // 2
    row, inw, outw = lax.axis_index("row"), lax.axis_index("inw"), lax.axis_index("outw")
    z, x = row // NX, row % NX
    y, core = outw * 4 + inw // 2, inw % 2
    s = 1 - 2 * core

    def dev(dz=0, dx=0, dy=0, other=False):
        zz, xx, yy = (z + dz + NZ) % NZ, (x + dx + NX) % NX, (y + dy + NY) % NY
        cc = 1 - core if other else core
        return (zz * NX + xx, (yy % 4) * 2 + cc, yy // 4)

    def at_y(k):
        return (y + k * s + NY) % NY

    def y_dev(k):
        return dev(dy=k * s)

    started, used = [], [0, 0]

    def send(src, dst, device):
        i = used[0]
        used[0] += 1
        copy = pltpu.make_async_remote_copy(
            src_ref=src, dst_ref=dst, send_sem=ssem.at[i], recv_sem=rsem.at[i], device_id=device, device_id_type=MESH
        )
        copy.start()
        started.append(copy)
        return copy

    def local(src, dst):
        i = used[1]
        used[1] += 1
        copy = pltpu.make_async_copy(src, dst, lsem.at[i])
        copy.start()
        return copy

    halves = [pl.ds(pl.multiple_of(h * f, f), f) for h in (core, 1 - core)]
    loads = []
    for h in range(2):
        loads.append(local(wg_hbm.at[:, halves[h]], buf["wg"].at[h]))
        loads.append(local(wu_hbm.at[:, halves[h]], buf["wu"].at[h]))
        loads.append(local(wd_hbm.at[halves[h], :], buf["wd"].at[h]))

    barrier = pltpu.get_barrier_semaphore()
    peers = [dev(dz=k) for k in range(1, NZ)] + [dev(dx=k) for k in range(1, NX)]
    peers += [dev(dy=k) for k in (1, -1, 2, -2)] + [dev(other=True)]
    for peer in peers:
        pl.semaphore_signal(barrier, inc=1, device_id=peer, device_id_type=MESH)
    xb, gb, hb = buf["xb"], buf["gb"], buf["hb"]
    xb[0, 0] = x_ref[...]
    gb[0, 0] = g_ref[...]
    pl.semaphore_wait(barrier, len(peers))

    got = {}
    near_first = (1, 7, 2, 6, 3, 5, 4)
    for k in near_first:
        got["zx", k] = send(x_ref, xb.at[0, k], dev(dz=k))
    for k in near_first:
        got["zg", k] = send(g_ref, gb.at[0, k], dev(dz=k))
    for copy in loads:
        copy.wait()

    def column(name, block):
        for k in near_first:
            got["z" + name, k].wait_recv()
        for c in (1, 3, 2):
            got["x" + name, c] = send(block.at[0], block.at[c], dev(dx=c))

    def products(c, g):
        for i, q in enumerate(GROUPS[c][g]):
            left = (gb if q == 2 else xb)[c].reshape(NZ * t, w)
            for h in (1, 0):
                if q == 2:
                    part = dot_nt(left, buf["wd"][h])
                else:
                    part = dot(left, buf["wu" if q else "wg"][h])
                to = buf[f"{'cs' if h else 'po'}{c}{g}"]
                to[:, i] = part.reshape(NZ, t, f)
        got["c", c, g] = send(buf[f"cs{c}{g}"], buf[f"cr{c}{g}"], dev(other=True))

    def arrive(c):
        got["xx", c].wait_recv()
        got["xg", c].wait_recv()

    def own(c, g, slot):
        return buf[f"po{c}{g}"][slot] + buf[f"cr{c}{g}"][slot]

    def leaf(c, g):
        got["c", c, g].wait_recv()
        pb, rr, ro = buf[f"pb{c}{g}"], buf[f"rr{c}{g}"], buf[f"ro{c}{g}"]
        for slot in range(NZ):
            pb[slot] = own(c, g, slot).astype(BF)
        got["l", c, g] = [
            send(pb.at[at_y(-3)], rr.at[0], y_dev(-1)),
            send(pb.at[at_y(-4)], rr.at[1], y_dev(-2)),
            send(pb.at[at_y(3)], rr.at[2], y_dev(1)),
        ]
        got["d", c, g] = [send(pb.at[at_y(-1)], ro.at[0], y_dev(-1)), send(pb.at[at_y(1)], ro.at[1], y_dev(1))]

    def relay(c, g):
        for copy in got["l", c, g]:
            copy.wait_recv()
        rr, sr, ro = buf[f"rr{c}{g}"], buf[f"sr{c}{g}"], buf[f"ro{c}{g}"]
        sr[0] = (own(c, g, at_y(-2)) + rr[0].astype(F32) + rr[1].astype(F32)).astype(BF)
        first = send(sr.at[0], ro.at[2], y_dev(-2))
        sr[1] = (own(c, g, at_y(2)) + rr[2].astype(F32)).astype(BF)
        got["d", c, g] += [first, send(sr.at[1], ro.at[3], y_dev(2))]

    def owner(c):
        sums = {}
        for g, qs in enumerate(GROUPS[c]):
            for copy in got["d", c, g]:
                copy.wait_recv()
            total = own(c, g, y)
            for i in range(4):
                total = total + buf[f"ro{c}{g}"][i].astype(F32)
            for i, q in enumerate(qs):
                sums[q] = total[i]
        gate, up, back = sums[0], sums[1], sums[2]
        sig = jax.nn.sigmoid(gate)
        silu = gate * sig
        hb[0, c, y, 0] = (back * up * sig * (1.0 + gate * (1.0 - sig))).astype(BF)
        hb[0, c, y, 1] = (back * silu).astype(BF)
        hb[0, c, y, 2] = (silu * up).astype(BF)

    def spread(c):
        mine = hb.at[0, c, y]
        for k in (2, -2, 1, -1):
            got["a", c, k] = send(mine, mine, y_dev(k))

    def pass_on(c):
        got["a", c, 2].wait_recv()
        block = hb.at[0, c, at_y(-2)]
        got["a", c, 4] = send(block, block, y_dev(2))
        got["a", c, 3] = send(block, block, y_dev(1))
        got["a", c, -2].wait_recv()
        block = hb.at[0, c, at_y(2)]
        got["a", c, -3] = send(block, block, y_dev(-1))

    def share(c):
        for k in (1, -1, 3, -3, 4):
            got["a", c, k].wait_recv()
        got["s", c] = send(hb.at[0, c], hb.at[1, c], dev(other=True))

    def back_product(c):
        got["s", c].wait_recv()
        total = None
        for h in range(2):
            for q, name in enumerate(("wg", "wu")):
                term = dot_nt(hb[h, c, :, q].reshape(NZ * t, f), buf[name][h])
                total = term if total is None else total + term
        buf["dxs"][c] = total.reshape(NZ, t, w)
        if c:
            got["dx", c] = send(buf["dxs"].at[c], buf["dxr"].at[c], dev(dx=-c))

    def reduce_inputs():
        for c in (1, 3, 2):
            got["dx", c].wait_recv()
        zs = buf["zs"]
        for k in (4, 3, 5, 2, 6, 1, 7):
            zs[k] = (buf["dxs"][0, k] + buf["dxr"][1, k] + buf["dxr"][2, k] + buf["dxr"][3, k]).astype(BF)
            got["zr", k] = send(zs.at[k], buf["zr"].at[k], dev(dz=-k))

    stores = []

    def weight_grads():
        left = xb[...].reshape(NX * NZ * t, w)
        for h in range(2):
            for q, name, out in ((0, "og", og_hbm), (1, "ou", ou_hbm)):
                right = hb[h, :, :, q].reshape(NX * NZ * t, f)
                buf[name][h] = dot_tn(left, right).astype(BF)
                stores.append(local(buf[name].at[h], out.at[:, halves[h]]))
        right = gb[...].reshape(NX * NZ * t, w)
        for h in range(2):
            left = hb[h, :, :, 2].reshape(NX * NZ * t, f)
            buf["od"][h] = dot_tn(left, right).astype(BF)
            stores.append(local(buf["od"].at[h], od_hbm.at[halves[h], :]))

    def finish():
        total = buf["dxs"][0, 0] + buf["dxr"][1, 0] + buf["dxr"][2, 0] + buf["dxr"][3, 0]
        for k in range(1, NZ):
            got["zr", k].wait_recv()
            total = total + buf["zr"][k].astype(F32)
        dx_ref[...] = total.astype(BF)

    column("x", xb)
    products(0, 0)
    leaf(0, 0)
    column("g", gb)
    products(0, 1)
    leaf(0, 1)
    relay(0, 0)
    relay(0, 1)
    arrive(1)
    products(1, 0)
    arrive(3)
    products(3, 0)
    owner(0)
    leaf(1, 0)
    leaf(3, 0)
    relay(1, 0)
    relay(3, 0)
    owner(1)
    spread(1)
    owner(3)
    spread(3)
    arrive(2)
    products(2, 0)
    leaf(2, 0)
    pass_on(1)
    pass_on(3)
    relay(2, 0)
    spread(0)
    share(1)
    share(3)
    back_product(1)
    owner(2)
    spread(2)
    back_product(3)
    pass_on(0)
    share(0)
    pass_on(2)
    back_product(0)
    share(2)
    back_product(2)
    reduce_inputs()
    weight_grads()
    finish()
    for copy in started:
        copy.wait_send()
    for copy in stores:
        copy.wait()


def per_device(inputs, out_grad, gate_weight, up_weight, down_weight):
    t, w = inputs.shape
    f = gate_weight.shape[1] // 2
    buffers = scratch(t, w, f)
    vmem, hbm = pl.BlockSpec(memory_space=pltpu.VMEM), pl.BlockSpec(memory_space=pl.ANY)
    flops = 2 * 8 * (NX * NZ * t) * w * (2 * f)
    return pl.pallas_call(
        functools.partial(kernel, list(buffers)),
        out_shape=(
            jax.ShapeDtypeStruct(inputs.shape, BF),
            jax.ShapeDtypeStruct(gate_weight.shape, BF),
            jax.ShapeDtypeStruct(up_weight.shape, BF),
            jax.ShapeDtypeStruct(down_weight.shape, BF),
        ),
        in_specs=[vmem, vmem, hbm, hbm, hbm],
        out_specs=(vmem, hbm, hbm, hbm),
        scratch_shapes=[pltpu.VMEM(shape, dtype) for shape, dtype in buffers.values()]
        + [
            pltpu.SemaphoreType.DMA((N_REMOTE,)),
            pltpu.SemaphoreType.DMA((N_REMOTE,)),
            pltpu.SemaphoreType.DMA((N_LOCAL,)),
        ],
        compiler_params=pltpu.CompilerParams(collective_id=0, has_side_effects=True, vmem_limit_bytes=56 << 20),
        cost_estimate=pl.CostEstimate(flops=flops, bytes_accessed=4 << 20, transcendentals=3 * NX * t * f),
    )(inputs, out_grad, gate_weight, up_weight, down_weight)


def solution(mesh):
    in_specs = (
        P("row", ("inw", "outw")),
        P("row", ("inw", "outw")),
        P(("inw", "outw"), "row"),
        P(("inw", "outw"), "row"),
        P("row", ("inw", "outw")),
    )
    out_specs = (
        P("row", ("inw", "outw")),
        P(("inw", "outw"), "row"),
        P(("inw", "outw"), "row"),
        P("row", ("inw", "outw")),
    )
    return jax.shard_map(per_device, mesh=mesh, in_specs=in_specs, out_specs=out_specs, check_vma=False)
```

time: 480 us -> 105 us (0.22)
  waiting for transfers between devices: 359 us -> 0 us
  Pallas kernels: 0 us -> 98.3 us
  blocking collectives: 81.8 us -> 0 us
  between operations: 14.1 us -> 0.64 us
  matrix products: 13.3 us -> 0 us
    reduce_scatter x1 -> x0, waiting for transfers between devices: 211 us -> none  [per_device(): lax.psum_scatter(contract_last(gate_grad, gate_weight) + contract_last(up...]
    psum x1 -> x0, waiting for transfers between devices: 148 us -> none  [per_device(): lax.psum((gate_part, up_part, back_part), ('inw', 'outw'))]
    pallas_call x0 -> x1, Pallas kernels: none -> 98.3 us  [per_device(): pl.pallas_call(functools.partial(kernel, list(buffers)), out_shape=(jax.S...]
    all_gather x2 -> x0, blocking collectives: 81.8 us -> none  [the longest x1 44.7 us: per_device(): lax.all_gather(inputs, 'row', axis=0, tiled=True)]
    dot_general x8 -> x0, matrix products: 13.3 us -> none  [the longest x3 5.65 us: contract_first(): lax.dot_general(left, right, (((0,), (0,)), ((), ())), preferred_element_...]
  transfers between devices with their start and end apart: 2 -> 0, of which waited for: 2 -> 0; matrix products, arithmetic and copies ran while one was open for 2% -> 0% of each run, Pallas kernels for 0% -> 0%
where the time goes in v1:
time: 105 us; the launch traced here: 104 us
  Pallas kernels  98.3 us (94%)
  local copies, waits for them, and re-layouts  5.3 us (5%)
    pallas_call x1, Pallas kernels, per_device(): pl.pallas_call(functools.partial(kernel, list(buffers)), out_shape=(jax.S...  98.3 us
    unnamed x8, local copies, waits for them, and re-layouts  5.3 us

profile of v1, /device:TPU:1, one launch (start us, length us, event | category | flops | bytes accessed | tf_op | source)
XLA Modules:
  0.0 104.2 jit_solution(11333930512388831476)
XLA Ops:
  0.6 98.3 %shard_map.84 = (bf16[24,512]{1,0:T(8,128)(2,1)}, bf16[512,512]{1,0:T(8,128)(2,1)}, bf16[512,512]{1,0:T(8,128)(2,1)}, bf16[512,512]{1,0:T(8,128)(2,1)}) custom-call(bf16[24,512]{1,0:T(8,128)(2,1)} %x_ref.1, bf16[24,512]{1,0:T(8,128)(2,1)} %g_ref.1, bf16[512,512]{1,0:T(8,128)(2,1)} %wg_hbm.1, bf16[512,512]{1,0:T(8,128)(2,1)} %wu_hbm.1, bf16[512,512]{1,0:T(8,128)(2,1)} %wd_hbm.1), custom_call_target="tpu_custom_call" | custom-call | flops 3221225472 | bytes 4194304 | tf_op jit(solution)/shard_map/pallas_call | solution.py:305
  98.9 1.3 %copy.13 = bf16[24,512]{1,0:T(8,128)(2,1)} copy(bf16[24,512]{1,0:T(8,128)(2,1)} %get-tuple-element.8) | data formatting | bytes 49152
  100.3 0.0 copy-start.1
  100.3 1.9 %copy.14 = bf16[512,512]{1,0:T(8,128)(2,1)} copy(bf16[512,512]{1,0:T(8,128)(2,1)} %get-tuple-element.9) | data formatting | bytes 1048576
  102.2 0.0 copy-done.1
  102.2 0.0 copy-start
  102.2 0.8 copy.15
  103.0 0.4 copy-done
  103.5 0.8 copy.16
Async XLA Ops:
  100.3 1.9 %copy-start.1 = (bf16[512,512]{1,0:T(8,128)(2,1)S(1)}, bf16[512,512]{1,0:T(8,128)(2,1)}, u32[]{:S(2)}) copy-start(bf16[512,512]{1,0:T(8,128)(2,1)} %get-tuple-element.10) | copy-start | bytes 1572868
  102.2 1.2 %copy-start = (bf16[512,512]{1,0:T(8,128)(2,1)S(1)}, bf16[512,512]{1,0:T(8,128)(2,1)}, u32[]{:S(2)}) copy-start(bf16[512,512]{1,0:T(8,128)(2,1)} %get-tuple-element.11) | copy-start | bytes 1572868

commit v2 on v1

--- a/solution.py
+++ b/solution.py
@@ -10,7 +10,7 @@
 MESH = pl.DeviceIdType.MESH
 BF, F32 = jnp.bfloat16, jnp.float32
 NZ, NX, NY = 8, 4, 8
-GROUPS = {0: ((0, 1), (2,)), 1: ((0, 1, 2),), 2: ((0, 1, 2),), 3: ((0, 1, 2),)}
+GROUPS = {c: ((0, 1), (2,)) for c in range(NX)}
 
 
 def dot(a, b):
@@ -32,11 +32,12 @@
         "wg": ((2, w, f), BF),
         "wu": ((2, w, f), BF),
         "wd": ((2, f, w), BF),
-        "hb": ((2, NX, NZ, 3, t, f), BF),
-        "dxs": ((NX, NZ, t, w), F32),
-        "dxr": ((NX, NZ, t, w), F32),
-        "zs": ((NZ, t, w), BF),
-        "zr": ((NZ, t, w), BF),
+        "hb": ((2, NX, NZ, 2, t, f), BF),
+        "hh": ((2, NY, NX, t, f), BF),
+        "dx": ((NX, t, w), F32),
+        "xr": ((NX, t, w), F32),
+        "zs": ((NX, NZ, t, w), BF),
+        "zr": ((NX, NZ, t, w), BF),
         "og": ((2, w, f), BF),
         "ou": ((2, w, f), BF),
         "od": ((2, f, w), BF),
@@ -54,7 +55,7 @@
     return made
 
 
-N_REMOTE = 160
+N_REMOTE = 256
 N_LOCAL = 16
 
 
@@ -110,25 +111,42 @@
     peers += [dev(dy=k) for k in (1, -1, 2, -2)] + [dev(other=True)]
     for peer in peers:
         pl.semaphore_signal(barrier, inc=1, device_id=peer, device_id_type=MESH)
-    xb, gb, hb = buf["xb"], buf["gb"], buf["hb"]
+    xb, gb, hb, hh = buf["xb"], buf["gb"], buf["hb"], buf["hh"]
     xb[0, 0] = x_ref[...]
     gb[0, 0] = g_ref[...]
     pl.semaphore_wait(barrier, len(peers))
 
     got = {}
-    near_first = (1, 7, 2, 6, 3, 5, 4)
-    for k in near_first:
-        got["zx", k] = send(x_ref, xb.at[0, k], dev(dz=k))
-    for k in near_first:
-        got["zg", k] = send(g_ref, gb.at[0, k], dev(dz=k))
-    for copy in loads:
-        copy.wait()
-
-    def column(name, block):
-        for k in near_first:
-            got["z" + name, k].wait_recv()
-        for c in (1, 3, 2):
-            got["x" + name, c] = send(block.at[0], block.at[c], dev(dx=c))
+    stores = []
+    blocks = {"x": (x_ref, xb), "g": (g_ref, gb)}
+
+    def first(name, c):
+        ref, block = blocks[name]
+        got[name, c, 0] = send(ref, block.at[c, 0], dev(dx=c))
+
+    def column(name):
+        ref, block = blocks[name]
+        for k in (1, 7, 2, 6, 3, 5, 4):
+            got[name, 0, k] = send(ref, block.at[0, k], dev(dz=k))
+
+    def forward(name, near):
+        block = blocks[name][1]
+        for k in (1, 7, 2, 6) if near else (3, 5, 4):
+            got[name, 0, k].wait_recv()
+        for start, size in ((1, 2), (6, 2)) if near else ((3, 3),):
+            for c in (1, 3):
+                part = pl.ds(start, size)
+                got[name, c, start] = send(block.at[0, part], block.at[c, part], dev(dx=c))
+
+    def across(name):
+        block = blocks[name][1]
+        got[name, 2, 0].wait_recv()
+        for k in (1, 7, 2, 6, 3, 5, 4):
+            got[name, 2, k] = send(block.at[2, 0], block.at[2, k], dev(dz=k))
+
+    def arrive(c, name):
+        for k in range(1, NZ) if c == 2 else (0, 1, 6, 3):
+            got[name, c, k].wait_recv()
 
     def products(c, g):
         for i, q in enumerate(GROUPS[c][g]):
@@ -142,10 +160,6 @@
                 to[:, i] = part.reshape(NZ, t, f)
         got["c", c, g] = send(buf[f"cs{c}{g}"], buf[f"cr{c}{g}"], dev(other=True))
 
-    def arrive(c):
-        got["xx", c].wait_recv()
-        got["xg", c].wait_recv()
-
     def own(c, g, slot):
         return buf[f"po{c}{g}"][slot] + buf[f"cr{c}{g}"][slot]
 
@@ -166,9 +180,9 @@
             copy.wait_recv()
         rr, sr, ro = buf[f"rr{c}{g}"], buf[f"sr{c}{g}"], buf[f"ro{c}{g}"]
         sr[0] = (own(c, g, at_y(-2)) + rr[0].astype(F32) + rr[1].astype(F32)).astype(BF)
-        first = send(sr.at[0], ro.at[2], y_dev(-2))
+        one = send(sr.at[0], ro.at[2], y_dev(-2))
         sr[1] = (own(c, g, at_y(2)) + rr[2].astype(F32)).astype(BF)
-        got["d", c, g] += [first, send(sr.at[1], ro.at[3], y_dev(2))]
+        got["d", c, g] += [one, send(sr.at[1], ro.at[3], y_dev(2))]
 
     def owner(c):
         sums = {}
@@ -185,26 +199,32 @@
         silu = gate * sig
         hb[0, c, y, 0] = (back * up * sig * (1.0 + gate * (1.0 - sig))).astype(BF)
         hb[0, c, y, 1] = (back * silu).astype(BF)
-        hb[0, c, y, 2] = (silu * up).astype(BF)
+        hh[0, y, c] = (silu * up).astype(BF)
+
+    def result(c, slot):
+        return hh.at[0, slot] if c == "h" else hb.at[0, c, slot]
 
     def spread(c):
-        mine = hb.at[0, c, y]
+        mine = result(c, y)
         for k in (2, -2, 1, -1):
             got["a", c, k] = send(mine, mine, y_dev(k))
 
     def pass_on(c):
         got["a", c, 2].wait_recv()
-        block = hb.at[0, c, at_y(-2)]
+        block = result(c, at_y(-2))
         got["a", c, 4] = send(block, block, y_dev(2))
         got["a", c, 3] = send(block, block, y_dev(1))
         got["a", c, -2].wait_recv()
-        block = hb.at[0, c, at_y(2)]
+        block = result(c, at_y(2))
         got["a", c, -3] = send(block, block, y_dev(-1))
 
     def share(c):
         for k in (1, -1, 3, -3, 4):
             got["a", c, k].wait_recv()
-        got["s", c] = send(hb.at[0, c], hb.at[1, c], dev(other=True))
+        if c == "h":
+            got["s", c] = send(hh.at[0], hh.at[1], dev(other=True))
+        else:
+            got["s", c] = send(hb.at[0, c], hb.at[1, c], dev(other=True))
 
     def back_product(c):
         got["s", c].wait_recv()
@@ -213,19 +233,24 @@
             for q, name in enumerate(("wg", "wu")):
                 term = dot_nt(hb[h, c, :, q].reshape(NZ * t, f), buf[name][h])
                 total = term if total is None else total + term
-        buf["dxs"][c] = total.reshape(NZ, t, w)
-        if c:
-            got["dx", c] = send(buf["dxs"].at[c], buf["dxr"].at[c], dev(dx=-c))
-
-    def reduce_inputs():
-        for c in (1, 3, 2):
-            got["dx", c].wait_recv()
-        zs = buf["zs"]
+        total = total.reshape(NZ, t, w)
+        zs, zr = buf["zs"], buf["zr"]
+        buf["dx"][c] = total[0]
+        for k in range(1, NZ):
+            zs[c, k] = total[k].astype(BF)
         for k in (4, 3, 5, 2, 6, 1, 7):
-            zs[k] = (buf["dxs"][0, k] + buf["dxr"][1, k] + buf["dxr"][2, k] + buf["dxr"][3, k]).astype(BF)
-            got["zr", k] = send(zs.at[k], buf["zr"].at[k], dev(dz=-k))
-
-    stores = []
+            got["zr", c, k] = send(zs.at[c, k], zr.at[c, k], dev(dz=-k))
+
+    def over_z(c):
+        total = buf["dx"][c]
+        for k in range(1, NZ):
+            got["zr", c, k].wait_recv()
+            total = total + buf["zr"][c, k].astype(F32)
+        return total
+
+    def over_x(c):
+        buf["dx"][c] = over_z(c)
+        got["xr", c] = send(buf["dx"].at[c], buf["xr"].at[c], dev(dx=-c))
 
     def weight_grads():
         left = xb[...].reshape(NX * NZ * t, w)
@@ -234,65 +259,116 @@
                 right = hb[h, :, :, q].reshape(NX * NZ * t, f)
                 buf[name][h] = dot_tn(left, right).astype(BF)
                 stores.append(local(buf[name].at[h], out.at[:, halves[h]]))
+
+    def down_grad():
         right = gb[...].reshape(NX * NZ * t, w)
+        got["s", "h"].wait_recv()
         for h in range(2):
-            left = hb[h, :, :, 2].reshape(NX * NZ * t, f)
+            left = jnp.concatenate([hh[h, :, c].reshape(NY * t, f) for c in range(NX)], axis=0)
             buf["od"][h] = dot_tn(left, right).astype(BF)
             stores.append(local(buf["od"].at[h], od_hbm.at[halves[h], :]))
 
     def finish():
-        total = buf["dxs"][0, 0] + buf["dxr"][1, 0] + buf["dxr"][2, 0] + buf["dxr"][3, 0]
-        for k in range(1, NZ):
-            got["zr", k].wait_recv()
-            total = total + buf["zr"][k].astype(F32)
+        total = over_z(0)
+        for c in range(1, NX):
+            got["xr", c].wait_recv()
+            total = total + buf["xr"][c]
         dx_ref[...] = total.astype(BF)
 
-    column("x", xb)
+    first("x", 2)
+    first("g", 2)
+    column("x")
+    first("x", 1)
+    first("x", 3)
+    column("g")
+    first("g", 1)
+    first("g", 3)
+    for copy in loads:
+        copy.wait()
+    forward("x", True)
+    forward("x", False)
+    across("x")
     products(0, 0)
     leaf(0, 0)
-    column("g", gb)
+    forward("g", True)
+    forward("g", False)
+    across("g")
     products(0, 1)
     leaf(0, 1)
-    relay(0, 0)
-    relay(0, 1)
-    arrive(1)
+    arrive(1, "x")
     products(1, 0)
-    arrive(3)
+    arrive(3, "x")
     products(3, 0)
-    owner(0)
     leaf(1, 0)
     leaf(3, 0)
+    relay(0, 0)
+    arrive(2, "x")
+    products(2, 0)
+    relay(0, 1)
+    leaf(2, 0)
+    arrive(1, "g")
+    products(1, 1)
+    arrive(3, "g")
+    products(3, 1)
     relay(1, 0)
+    leaf(1, 1)
     relay(3, 0)
+    leaf(3, 1)
+    owner(0)
+    spread(0)
+    arrive(2, "g")
+    products(2, 1)
+    relay(2, 0)
+    leaf(2, 1)
+    relay(1, 1)
+    relay(3, 1)
     owner(1)
     spread(1)
     owner(3)
     spread(3)
-    arrive(2)
-    products(2, 0)
-    leaf(2, 0)
+    pass_on(0)
+    relay(2, 1)
+    share(0)
+    owner(2)
+    spread(2)
+    back_product(0)
     pass_on(1)
     pass_on(3)
-    relay(2, 0)
-    spread(0)
+    spread("h")
     share(1)
+    back_product(1)
     share(3)
-    back_product(1)
-    owner(2)
-    spread(2)
     back_product(3)
-    pass_on(0)
-    share(0)
     pass_on(2)
-    back_product(0)
     share(2)
     back_product(2)
-    reduce_inputs()
+    pass_on("h")
     weight_grads()
+    over_x(1)
+    over_x(3)
+    over_x(2)
+    share("h")
+    down_grad()
     finish()
     for copy in started:
         copy.wait_send()
     for copy in stores:
+        copy.wait()
+
+
+def copies(*refs):
+    sem = refs[-1]
+    n = len(refs) // 2
+    started = []
+    for i in range(n):
+        src, dst = refs[i], refs[n + i]
+        parts = 8 if src.shape[0] % 128 == 0 else 1
+        rows = src.shape[0] // parts
+        for p in range(parts):
+            part = pl.ds(p * rows, rows)
+            started.append(pltpu.make_async_copy(src.at[part], dst.at[part], sem.at[len(started)]))
+            started[-1].start()
+    for copy in started:
         copy.wait()
 
 
@@ -302,7 +378,7 @@
     buffers = scratch(t, w, f)
     vmem, hbm = pl.BlockSpec(memory_space=pltpu.VMEM), pl.BlockSpec(memory_space=pl.ANY)
     flops = 2 * 8 * (NX * NZ * t) * w * (2 * f)
-    return pl.pallas_call(
+    made = pl.pallas_call(
         functools.partial(kernel, list(buffers)),
         out_shape=(
             jax.ShapeDtypeStruct(inputs.shape, BF),
@@ -321,6 +397,14 @@
         compiler_params=pltpu.CompilerParams(collective_id=0, has_side_effects=True, vmem_limit_bytes=56 << 20),
         cost_estimate=pl.CostEstimate(flops=flops, bytes_accessed=4 << 20, transcendentals=3 * NX * t * f),
     )(inputs, out_grad, gate_weight, up_weight, down_weight)
+    return pl.pallas_call(
+        copies,
+        out_shape=tuple(jax.ShapeDtypeStruct(a.shape, a.dtype) for a in made),
+        in_specs=[hbm] * 4,
+        out_specs=(hbm,) * 4,
+        scratch_shapes=[pltpu.SemaphoreType.DMA((32,))],
+        cost_estimate=pl.CostEstimate(flops=0, bytes_accessed=4 << 20, transcendentals=0),
+    )(*made)
 
 
 def solution(mesh):

time: 105 us -> 137 us (1.30)
  Pallas kernels: 98.3 us -> 136 us
  local copies, waits for them, and re-layouts: 5.3 us -> 0 us
    pallas_call x0 -> x1, Pallas kernels: none -> 49.8 us  [per_device(): pl.pallas_call(copies, out_shape=tuple((jax.ShapeDtypeStruct(a.shape, a.d...]
    pallas_call x1, Pallas kernels: 98.3 us -> 86.6 us  [per_device(): pl.pallas_call(functools.partial(kernel, list(buffers)), out_shape=(jax.S...]
    unnamed x8 -> x0, local copies, waits for them, and re-layouts: 5.3 us -> none
where the time goes in v2:
time: 137 us
  Pallas kernels  136 us (99%)
    pallas_call x1, Pallas kernels, per_device(): pl.pallas_call(functools.partial(kernel, list(buffers)), out_shape=(jax.S...  86.6 us
    pallas_call x1, Pallas kernels, per_device(): pl.pallas_call(copies, out_shape=tuple((jax.ShapeDtypeStruct(a.shape, a.d...  49.8 us

profile of v2, /device:TPU:1, one launch (start us, length us, event | category | flops | bytes accessed | tf_op | source)
XLA Modules:
  0.0 137.0 jit_solution(4417538378916697923)
XLA Ops:
  0.6 86.6 %shard_map.84 = (bf16[24,512]{1,0:T(8,128)(2,1)}, bf16[512,512]{1,0:T(8,128)(2,1)}, bf16[512,512]{1,0:T(8,128)(2,1)}, bf16[512,512]{1,0:T(8,128)(2,1)}) custom-call(bf16[24,512]{1,0:T(8,128)(2,1)} %x_ref.1, bf16[24,512]{1,0:T(8,128)(2,1)} %g_ref.1, bf16[512,512]{1,0:T(8,128)(2,1)} %wg_hbm.1, bf16[512,512]{1,0:T(8,128)(2,1)} %wu_hbm.1, bf16[512,512]{1,0:T(8,128)(2,1)} %wd_hbm.1), custom_call_target="tpu_custom_call" | custom-call | flops 3221225472 | bytes 4194304 | tf_op jit(solution)/shard_map/pallas_call | solution.py:381
  87.2 49.8 %shard_map.85 = (bf16[24,512]{1,0:T(8,128)(2,1)}, bf16[512,512]{1,0:T(8,128)(2,1)}, bf16[512,512]{1,0:T(8,128)(2,1)}, bf16[512,512]{1,0:T(8,128)(2,1)}) custom-call(bf16[24,512]{1,0:T(8,128)(2,1)} %get-tuple-element.8.refs_0_, bf16[512,512]{1,0:T(8,128)(2,1)} %get-tuple-element.9.refs_1_, bf16[512,512]{1,0:T(8,128)(2,1)} %get-tuple-element.10.refs_2_, ...), custom_call_target="tpu_custom_call" | custom-call | bytes 4194304 | tf_op jit(solution)/shard_map/pallas_call | solution.py:400

commit v3 on v2

--- a/solution.py
+++ b/solution.py
@@ -36,6 +36,9 @@
         "hh": ((2, NY, NX, t, f), BF),
         "dx": ((NX, t, w), F32),
         "xr": ((NX, t, w), F32),
+        "d0": ((NZ, t, w), F32),
+        "xs": ((NX, NZ, t, w), BF),
+        "xq": ((NX, NZ, t, w), BF),
         "zs": ((NX, NZ, t, w), BF),
         "zr": ((NX, NZ, t, w), BF),
         "og": ((2, w, f), BF),
@@ -149,6 +152,9 @@
             got[name, c, k].wait_recv()
 
     def products(c, g):
+        if c:
+            for name in sorted({"g" if q == 2 else "x" for q in GROUPS[c][g]}):
+                arrive(c, name)
         for i, q in enumerate(GROUPS[c][g]):
             left = (gb if q == 2 else xb)[c].reshape(NZ * t, w)
             for h in (1, 0):
@@ -234,12 +240,26 @@
                 term = dot_nt(hb[h, c, :, q].reshape(NZ * t, f), buf[name][h])
                 total = term if total is None else total + term
         total = total.reshape(NZ, t, w)
+        if c in (1, 3):
+            buf["xs"][c] = total.astype(BF)
+            got["xq", c] = send(buf["xs"].at[c], buf["xq"].at[c], dev(dx=-c))
+        elif c == 0:
+            buf["d0"][...] = total
+        else:
+            to_z(c, lambda k: total[k])
+
+    def to_z(c, block):
         zs, zr = buf["zs"], buf["zr"]
-        buf["dx"][c] = total[0]
-        for k in range(1, NZ):
-            zs[c, k] = total[k].astype(BF)
         for k in (4, 3, 5, 2, 6, 1, 7):
+            zs[c, k] = block(k).astype(BF)
             got["zr", c, k] = send(zs.at[c, k], zr.at[c, k], dev(dz=-k))
+        buf["dx"][c] = block(0)
+
+    def mix():
+        for c in (1, 3):
+            got["xq", c].wait_recv()
+        xq = buf["xq"]
+        to_z(0, lambda k: buf["d0"][k] + xq[1, k].astype(F32) + xq[3, k].astype(F32))
 
     def over_z(c):
         total = buf["dx"][c]
@@ -270,9 +290,8 @@
 
     def finish():
         total = over_z(0)
-        for c in range(1, NX):
-            got["xr", c].wait_recv()
-            total = total + buf["xr"][c]
+        got["xr", 2].wait_recv()
+        total = total + buf["xr"][2]
         dx_ref[...] = total.astype(BF)
 
     first("x", 2)
@@ -285,67 +304,60 @@
     first("g", 3)
     for copy in loads:
         copy.wait()
+    across("x")
     forward("x", True)
     forward("x", False)
-    across("x")
+    across("g")
     products(0, 0)
     leaf(0, 0)
     forward("g", True)
     forward("g", False)
-    across("g")
     products(0, 1)
+    products(1, 0)
+    products(3, 0)
     leaf(0, 1)
-    arrive(1, "x")
-    products(1, 0)
-    arrive(3, "x")
-    products(3, 0)
     leaf(1, 0)
+    relay(0, 0)
+    products(2, 0)
     leaf(3, 0)
-    relay(0, 0)
-    arrive(2, "x")
-    products(2, 0)
+    products(1, 1)
+    products(3, 1)
     relay(0, 1)
+    leaf(1, 1)
+    leaf(3, 1)
+    products(2, 1)
     leaf(2, 0)
-    arrive(1, "g")
-    products(1, 1)
-    arrive(3, "g")
-    products(3, 1)
+    leaf(2, 1)
     relay(1, 0)
-    leaf(1, 1)
+    relay(1, 1)
     relay(3, 0)
-    leaf(3, 1)
     owner(0)
+    relay(3, 1)
+    relay(2, 0)
+    relay(2, 1)
     spread(0)
-    arrive(2, "g")
-    products(2, 1)
-    relay(2, 0)
-    leaf(2, 1)
-    relay(1, 1)
-    relay(3, 1)
     owner(1)
     spread(1)
     owner(3)
     spread(3)
-    pass_on(0)
-    relay(2, 1)
-    share(0)
     owner(2)
     spread(2)
-    back_product(0)
     pass_on(1)
     pass_on(3)
-    spread("h")
+    pass_on(2)
+    pass_on(0)
     share(1)
     back_product(1)
     share(3)
+    spread("h")
+    share(2)
     back_product(3)
-    pass_on(2)
-    share(2)
+    share(0)
     back_product(2)
+    back_product(0)
+    weight_grads()
     pass_on("h")
-    weight_grads()
-    over_x(1)
-    over_x(3)
+    mix()
     over_x(2)
     share("h")
     down_grad()
@@ -357,19 +369,22 @@
 
 
 def copies(*refs):
-    sem = refs[-1]
-    n = len(refs) // 2
-    started = []
-    for i in range(n):
-        src, dst = refs[i], refs[n + i]
-        parts = 8 if src.shape[0] % 128 == 0 else 1
-        rows = src.shape[0] // parts
-        for p in range(parts):
-            part = pl.ds(p * rows, rows)
-            started.append(pltpu.make_async_copy(src.at[part], dst.at[part], sem.at[len(started)]))
-            started[-1].start()
-    for copy in started:
-        copy.wait()
+    n = len(refs) // 3
+    came, went = refs[3 * n :]
+    parts = []
+    for src, dst, held in zip(refs[:n], refs[n : 2 * n], refs[2 * n : 3 * n]):
+        pieces = 4 if src.shape[0] % 64 == 0 else 1
+        rows = src.shape[0] // pieces
+        for p in range(pieces):
+            part, i = pl.ds(p * rows, rows), len(parts)
+            inward = pltpu.make_async_copy(src.at[part], held.at[part], came.at[i])
+            parts.append((inward, pltpu.make_async_copy(held.at[part], dst.at[part], went.at[i])))
+            inward.start()
+    for inward, outward in parts:
+        inward.wait()
+        outward.start()
+    for inward, outward in parts:
+        outward.wait()
 
 
 def per_device(inputs, out_grad, gate_weight, up_weight, down_weight):
@@ -402,7 +417,8 @@
         out_shape=tuple(jax.ShapeDtypeStruct(a.shape, a.dtype) for a in made),
         in_specs=[hbm] * 4,
         out_specs=(hbm,) * 4,
-        scratch_shapes=[pltpu.SemaphoreType.DMA((32,))],
+        scratch_shapes=[pltpu.VMEM(a.shape, a.dtype) for a in made]
+        + [pltpu.SemaphoreType.DMA((16,)), pltpu.SemaphoreType.DMA((16,))],
         cost_estimate=pl.CostEstimate(flops=0, bytes_accessed=4 << 20, transcendentals=0),
     )(*made)
 

time: 137 us -> 79.3 us (0.58)
  Pallas kernels: 136 us -> 78.5 us
    pallas_call x1, Pallas kernels: 49.8 us -> 2.41 us  [per_device(): pl.pallas_call(copies, out_shape=tuple((jax.ShapeDtypeStruct(a.shape, a.d...]
    pallas_call x1, Pallas kernels: 86.6 us -> 76.1 us  [per_device(): pl.pallas_call(functools.partial(kernel, list(buffers)), out_shape=(jax.S...]
where the time goes in v3:
time: 79.3 us; the launch traced here: 79.1 us
  Pallas kernels  78.5 us (99%)
    pallas_call x1, Pallas kernels, per_device(): pl.pallas_call(functools.partial(kernel, list(buffers)), out_shape=(jax.S...  76.1 us
    pallas_call x1, Pallas kernels, per_device(): pl.pallas_call(copies, out_shape=tuple((jax.ShapeDtypeStruct(a.shape, a.d...  2.41 us

profile of v3, /device:TPU:1, one launch (start us, length us, event | category | flops | bytes accessed | tf_op | source)
XLA Modules:
  0.0 79.1 jit_solution(11562697308372032457)
XLA Ops:
  0.6 76.1 %shard_map.84 = (bf16[24,512]{1,0:T(8,128)(2,1)}, bf16[512,512]{1,0:T(8,128)(2,1)}, bf16[512,512]{1,0:T(8,128)(2,1)}, bf16[512,512]{1,0:T(8,128)(2,1)}) custom-call(bf16[24,512]{1,0:T(8,128)(2,1)} %x_ref.1, bf16[24,512]{1,0:T(8,128)(2,1)} %g_ref.1, bf16[512,512]{1,0:T(8,128)(2,1)} %wg_hbm.1, bf16[512,512]{1,0:T(8,128)(2,1)} %wu_hbm.1, bf16[512,512]{1,0:T(8,128)(2,1)} %wd_hbm.1), custom_call_target="tpu_custom_call" | custom-call | flops 3221225472 | bytes 4194304 | tf_op jit(solution)/shard_map/pallas_call | solution.py:396
  76.7 2.4 %shard_map.85 = (bf16[24,512]{1,0:T(8,128)(2,1)}, bf16[512,512]{1,0:T(8,128)(2,1)}, bf16[512,512]{1,0:T(8,128)(2,1)}, bf16[512,512]{1,0:T(8,128)(2,1)}) custom-call(bf16[24,512]{1,0:T(8,128)(2,1)} %get-tuple-element.8.refs_0_, bf16[512,512]{1,0:T(8,128)(2,1)} %get-tuple-element.9.refs_1_, bf16[512,512]{1,0:T(8,128)(2,1)} %get-tuple-element.10.refs_2_, ...), custom_call_target="tpu_custom_call" | custom-call | bytes 4194304 | tf_op jit(solution)/shard_map/pallas_call | solution.py:415

commit v4 on v3

--- a/solution.py
+++ b/solution.py
@@ -41,9 +41,6 @@
         "xq": ((NX, NZ, t, w), BF),
         "zs": ((NX, NZ, t, w), BF),
         "zr": ((NX, NZ, t, w), BF),
-        "og": ((2, w, f), BF),
-        "ou": ((2, w, f), BF),
-        "od": ((2, f, w), BF),
     }
     for c, groups in GROUPS.items():
         for g, qs in enumerate(groups):
@@ -62,7 +59,7 @@
 N_LOCAL = 16
 
 
-def kernel(names, x_ref, g_ref, wg_hbm, wu_hbm, wd_hbm, dx_ref, og_hbm, ou_hbm, od_hbm, *refs):
+def kernel(names, x_ref, g_ref, wg_hbm, wu_hbm, wd_hbm, dx_ref, og_ref, ou_ref, od_ref, *refs):
     buf = dict(zip(names, refs))
     ssem, rsem, lsem = refs[len(names) :]
     t, w = x_ref.shape
@@ -120,7 +117,6 @@
     pl.semaphore_wait(barrier, len(peers))
 
     got = {}
-    stores = []
     blocks = {"x": (x_ref, xb), "g": (g_ref, gb)}
 
     def first(name, c):
@@ -129,7 +125,7 @@
 
     def column(name):
         ref, block = blocks[name]
-        for k in (1, 7, 2, 6, 3, 5, 4):
+        for k in (4, 3, 5, 2, 6, 1, 7):
             got[name, 0, k] = send(ref, block.at[0, k], dev(dz=k))
 
     def forward(name, near):
@@ -144,7 +140,7 @@
     def across(name):
         block = blocks[name][1]
         got[name, 2, 0].wait_recv()
-        for k in (1, 7, 2, 6, 3, 5, 4):
+        for k in (4, 3, 5, 2, 6, 1, 7):
             got[name, 2, k] = send(block.at[2, 0], block.at[2, k], dev(dz=k))
 
     def arrive(c, name):
@@ -275,18 +271,16 @@
     def weight_grads():
         left = xb[...].reshape(NX * NZ * t, w)
         for h in range(2):
-            for q, name, out in ((0, "og", og_hbm), (1, "ou", ou_hbm)):
+            for q, out in ((0, og_ref), (1, ou_ref)):
                 right = hb[h, :, :, q].reshape(NX * NZ * t, f)
-                buf[name][h] = dot_tn(left, right).astype(BF)
-                stores.append(local(buf[name].at[h], out.at[:, halves[h]]))
+                out[:, halves[h]] = dot_tn(left, right).astype(BF)
 
     def down_grad():
         right = gb[...].reshape(NX * NZ * t, w)
         got["s", "h"].wait_recv()
         for h in range(2):
             left = jnp.concatenate([hh[h, :, c].reshape(NY * t, f) for c in range(NX)], axis=0)
-            buf["od"][h] = dot_tn(left, right).astype(BF)
-            stores.append(local(buf["od"].at[h], od_hbm.at[halves[h], :]))
+            od_ref[halves[h], :] = dot_tn(left, right).astype(BF)
 
     def finish():
         total = over_z(0)
@@ -305,34 +299,34 @@
     for copy in loads:
         copy.wait()
     across("x")
+    across("g")
+    forward("x", False)
     forward("x", True)
-    forward("x", False)
-    across("g")
     products(0, 0)
     leaf(0, 0)
+    forward("g", False)
     forward("g", True)
-    forward("g", False)
     products(0, 1)
     products(1, 0)
+    leaf(0, 1)
+    relay(0, 0)
     products(3, 0)
-    leaf(0, 1)
     leaf(1, 0)
-    relay(0, 0)
-    products(2, 0)
     leaf(3, 0)
     products(1, 1)
     products(3, 1)
+    products(2, 0)
     relay(0, 1)
     leaf(1, 1)
+    products(2, 1)
     leaf(3, 1)
-    products(2, 1)
     leaf(2, 0)
     leaf(2, 1)
     relay(1, 0)
     relay(1, 1)
-    relay(3, 0)
     owner(0)
     relay(3, 1)
+    relay(3, 0)
     relay(2, 0)
     relay(2, 1)
     spread(0)
@@ -343,48 +337,36 @@
     owner(2)
     spread(2)
     pass_on(1)
+    pass_on(0)
     pass_on(3)
     pass_on(2)
-    pass_on(0)
+    spread("h")
     share(1)
     back_product(1)
     share(3)
-    spread("h")
     share(2)
+    share(0)
     back_product(3)
-    share(0)
     back_product(2)
     back_product(0)
     weight_grads()
     pass_on("h")
     mix()
+    share("h")
     over_x(2)
-    share("h")
     down_grad()
     finish()
     for copy in started:
         copy.wait_send()
-    for copy in stores:
+
+
+def copies(*refs):
+    n, sem = len(refs) // 2, refs[-1]
+    started = [pltpu.make_async_copy(refs[i], refs[n + i], sem.at[i]) for i in range(n)]
+    for copy in started:
+        copy.start()
+    for copy in started:
         copy.wait()
-
-
-def copies(*refs):
-    n = len(refs) // 3
-    came, went = refs[3 * n :]
-    parts = []
-    for src, dst, held in zip(refs[:n], refs[n : 2 * n], refs[2 * n : 3 * n]):
-        pieces = 4 if src.shape[0] % 64 == 0 else 1
-        rows = src.shape[0] // pieces
-        for p in range(pieces):
-            part, i = pl.ds(p * rows, rows), len(parts)
-            inward = pltpu.make_async_copy(src.at[part], held.at[part], came.at[i])
-            parts.append((inward, pltpu.make_async_copy(held.at[part], dst.at[part], went.at[i])))
-            inward.start()
-    for inward, outward in parts:
-        inward.wait()
-        outward.start()
-    for inward, outward in parts:
-        outward.wait()
 
 
 def per_device(inputs, out_grad, gate_weight, up_weight, down_weight):
@@ -396,13 +378,13 @@
     made = pl.pallas_call(
         functools.partial(kernel, list(buffers)),
         out_shape=(
-            jax.ShapeDtypeStruct(inputs.shape, BF),
-            jax.ShapeDtypeStruct(gate_weight.shape, BF),
-            jax.ShapeDtypeStruct(up_weight.shape, BF),
-            jax.ShapeDtypeStruct(down_weight.shape, BF),
+            pltpu.VMEM(inputs.shape, BF),
+            pltpu.VMEM(gate_weight.shape, BF),
+            pltpu.VMEM(up_weight.shape, BF),
+            pltpu.VMEM(down_weight.shape, BF),
         ),
         in_specs=[vmem, vmem, hbm, hbm, hbm],
-        out_specs=(vmem, hbm, hbm, hbm),
+        out_specs=(vmem,) * 4,
         scratch_shapes=[pltpu.VMEM(shape, dtype) for shape, dtype in buffers.values()]
         + [
             pltpu.SemaphoreType.DMA((N_REMOTE,)),
@@ -415,13 +397,11 @@
     return pl.pallas_call(
         copies,
         out_shape=tuple(jax.ShapeDtypeStruct(a.shape, a.dtype) for a in made),
-        in_specs=[hbm] * 4,
+        in_specs=[vmem] * 4,
         out_specs=(hbm,) * 4,
-        scratch_shapes=[pltpu.VMEM(a.shape, a.dtype) for a in made]
-        + [pltpu.SemaphoreType.DMA((16,)), pltpu.SemaphoreType.DMA((16,))],
+        scratch_shapes=[pltpu.SemaphoreType.DMA((4,))],
         cost_estimate=pl.CostEstimate(flops=0, bytes_accessed=4 << 20, transcendentals=0),
-    )(*made)
-
+    )(*(pltpu.with_memory_space_constraint(a, pltpu.VMEM) for a in made))
 
 def solution(mesh):
     in_specs = (

time: 79.3 us -> 77.5 us (0.977)
  Pallas kernels: 78.5 us -> 76.6 us
    pallas_call x1, Pallas kernels: 2.41 us -> 1.18 us  [per_device(): pl.pallas_call(copies, out_shape=tuple((jax.ShapeDtypeStruct(a.shape, a.d...]
where the time goes in v4:
time: 77.5 us; the launch traced here: 77.3 us
  Pallas kernels  76.6 us (99%)
    pallas_call x1, Pallas kernels, per_device(): pl.pallas_call(functools.partial(kernel, list(buffers)), out_shape=(pltpu...  75.5 us

profile of v4, /device:TPU:1, one launch (start us, length us, event | category | flops | bytes accessed | tf_op | source)
XLA Modules:
  0.0 77.3 jit_solution(16500109362379854622)
XLA Ops:
  0.6 75.5 %shard_map.84 = (bf16[24,512]{1,0:T(8,128)(2,1)S(1)}, bf16[512,512]{1,0:T(8,128)(2,1)S(1)}, bf16[512,512]{1,0:T(8,128)(2,1)S(1)}, bf16[512,512]{1,0:T(8,128)(2,1)S(1)}) custom-call(bf16[24,512]{1,0:T(8,128)(2,1)} %x_ref.1, bf16[24,512]{1,0:T(8,128)(2,1)} %g_ref.1, bf16[512,512]{1,0:T(8,128)(2,1)} %wg_hbm.1, bf16[512,512]{1,0:T(8,128)(2,1)} %wu_hbm.1, ...), custom_call_target="tpu_custom_call" | custom-call | flops 3221225472 | bytes 4194304 | tf_op jit(solution)/shard_map/pallas_call | solution.py:378
  76.1 1.2 %shard_map.85 = (bf16[24,512]{1,0:T(8,128)(2,1)}, bf16[512,512]{1,0:T(8,128)(2,1)}, bf16[512,512]{1,0:T(8,128)(2,1)}, bf16[512,512]{1,0:T(8,128)(2,1)}) custom-call(bf16[24,512]{1,0:T(8,128)(2,1)S(1)} %get-tuple-element.8.refs_0_, bf16[512,512]{1,0:T(8,128)(2,1)S(1)} %get-tuple-element.9.refs_1_, bf16[512,512]{1,0:T(8,128)(2,1)S(1)} %get-tuple-element.10.refs_2_, ...), custom_call_target="tpu_custom_call" | custom-call | bytes 4194304 | tf_op jit(solution)/shard_map/pallas_call | solution.py:397

commit v5 on v4

--- a/solution.py
+++ b/solution.py
@@ -56,6 +56,7 @@
 
 
 N_REMOTE = 256
+PARTS = ((3, 3), (6, 2), (0, 3))
 N_LOCAL = 16
 
 
@@ -238,24 +239,29 @@
         total = total.reshape(NZ, t, w)
         if c in (1, 3):
             buf["xs"][c] = total.astype(BF)
-            got["xq", c] = send(buf["xs"].at[c], buf["xq"].at[c], dev(dx=-c))
+            for start, size in PARTS:
+                part = pl.ds(start, size)
+                got["xq", c, start] = send(buf["xs"].at[c, part], buf["xq"].at[c, part], dev(dx=-c))
         elif c == 0:
             buf["d0"][...] = total
         else:
-            to_z(c, lambda k: total[k])
-
-    def to_z(c, block):
+            to_z(c, lambda k: total[k], (4, 3, 5, 2, 6, 1, 7))
+
+    def to_z(c, block, order):
         zs, zr = buf["zs"], buf["zr"]
-        for k in (4, 3, 5, 2, 6, 1, 7):
+        for k in order:
             zs[c, k] = block(k).astype(BF)
             got["zr", c, k] = send(zs.at[c, k], zr.at[c, k], dev(dz=-k))
-        buf["dx"][c] = block(0)
-
-    def mix():
+        if 1 in order:
+            buf["dx"][c] = block(0)
+
+    def mix(far):
         for c in (1, 3):
-            got["xq", c].wait_recv()
+            for start, _ in PARTS[:1] if far else PARTS[1:]:
+                got["xq", c, start].wait_recv()
         xq = buf["xq"]
-        to_z(0, lambda k: buf["d0"][k] + xq[1, k].astype(F32) + xq[3, k].astype(F32))
+        order = (4, 3, 5) if far else (2, 6, 1, 7)
+        to_z(0, lambda k: buf["d0"][k] + xq[1, k].astype(F32) + xq[3, k].astype(F32), order)
 
     def over_z(c):
         total = buf["dx"][c]
@@ -287,6 +293,10 @@
         got["xr", 2].wait_recv()
         total = total + buf["xr"][2]
         dx_ref[...] = total.astype(BF)
+
+    def settle():
+        while started:
+            started.pop().wait_send()
 
     first("x", 2)
     first("g", 2)
@@ -298,14 +308,14 @@
     first("g", 3)
     for copy in loads:
         copy.wait()
-    across("x")
-    across("g")
     forward("x", False)
     forward("x", True)
     products(0, 0)
+    across("x")
     leaf(0, 0)
     forward("g", False)
     forward("g", True)
+    across("g")
     products(0, 1)
     products(1, 0)
     leaf(0, 1)
@@ -318,15 +328,15 @@
     products(2, 0)
     relay(0, 1)
     leaf(1, 1)
+    leaf(3, 1)
     products(2, 1)
-    leaf(3, 1)
     leaf(2, 0)
     leaf(2, 1)
     relay(1, 0)
     relay(1, 1)
     owner(0)
+    relay(3, 0)
     relay(3, 1)
-    relay(3, 0)
     relay(2, 0)
     relay(2, 1)
     spread(0)
@@ -337,27 +347,27 @@
     owner(2)
     spread(2)
     pass_on(1)
-    pass_on(0)
     pass_on(3)
     pass_on(2)
-    spread("h")
+    pass_on(0)
     share(1)
     back_product(1)
     share(3)
+    spread("h")
     share(2)
-    share(0)
     back_product(3)
     back_product(2)
+    share(0)
+    pass_on("h")
     back_product(0)
+    mix(True)
+    mix(False)
+    over_x(2)
+    share("h")
     weight_grads()
-    pass_on("h")
-    mix()
-    share("h")
-    over_x(2)
     down_grad()
+    settle()
     finish()
-    for copy in started:
-        copy.wait_send()
 
 
 def copies(*refs):

time: 77.5 us -> 74.7 us (0.964)
  Pallas kernels: 76.6 us -> 73.9 us
    pallas_call x1, Pallas kernels: 75.5 us -> 72.7 us  [per_device(): pl.pallas_call(functools.partial(kernel, list(buffers)), out_shape=(pltpu...]
where the time goes in v5:
time: 74.7 us; the launch traced here: 74.5 us
  Pallas kernels  73.9 us (99%)
    pallas_call x1, Pallas kernels, per_device(): pl.pallas_call(functools.partial(kernel, list(buffers)), out_shape=(pltpu...  72.7 us

profile of v5, /device:TPU:1, one launch (start us, length us, event | category | flops | bytes accessed | tf_op | source)
XLA Modules:
  0.0 74.5 jit_solution(11264053756836973468)
XLA Ops:
  0.6 72.7 %shard_map.84 = (bf16[24,512]{1,0:T(8,128)(2,1)S(1)}, bf16[512,512]{1,0:T(8,128)(2,1)S(1)}, bf16[512,512]{1,0:T(8,128)(2,1)S(1)}, bf16[512,512]{1,0:T(8,128)(2,1)S(1)}) custom-call(bf16[24,512]{1,0:T(8,128)(2,1)} %x_ref.1, bf16[24,512]{1,0:T(8,128)(2,1)} %g_ref.1, bf16[512,512]{1,0:T(8,128)(2,1)} %wg_hbm.1, bf16[512,512]{1,0:T(8,128)(2,1)} %wu_hbm.1, ...), custom_call_target="tpu_custom_call" | custom-call | flops 3221225472 | bytes 4194304 | tf_op jit(solution)/shard_map/pallas_call | solution.py:388
  73.4 1.2 %shard_map.85 = (bf16[24,512]{1,0:T(8,128)(2,1)}, bf16[512,512]{1,0:T(8,128)(2,1)}, bf16[512,512]{1,0:T(8,128)(2,1)}, bf16[512,512]{1,0:T(8,128)(2,1)}) custom-call(bf16[24,512]{1,0:T(8,128)(2,1)S(1)} %get-tuple-element.8.refs_0_, bf16[512,512]{1,0:T(8,128)(2,1)S(1)} %get-tuple-element.9.refs_1_, bf16[512,512]{1,0:T(8,128)(2,1)S(1)} %get-tuple-element.10.refs_2_, ...), custom_call_target="tpu_custom_call" | custom-call | bytes 4194304 | tf_op jit(solution)/shard_map/pallas_call | solution.py:407
